TPU v7x, 32 devices: a whole 2x2x4 slice. The times are simulated.
32 devices in a mesh: dev: 32 (over z, y, x, core).
Axes of the slice: x: 2, y: 2, z: 4, core: 2. Of those that a mesh axis runs over, the one named last changes fastest.
Arguments:
- queries: bfloat16 [64, 32, 128], P('dev'), may hold values from -0.119628906 to 0.119628906
- passages: bfloat16 [16384, 64, 128], P('dev'), may hold values from -1.796875 to 1.796875
- lengths: int32 [16384], P('dev'), may hold values from 16 to 64
- candidates: int32 [64, 64], P('dev'), may hold values from 0 to 16383, as said below
Outputs:
- scores: float32 [64, 64], P('dev')
Inputs may be any that keep to these rules, and one draw needn't show every extreme that they name: `candidates`: the 128 entries of the rows held by one device name, with repetition, at most 8 passages held by any one device (passage p is held by device p // 512), and exactly 8 for four devices; the passages of low number within each device are named far more often than the others, and a few devices are named far more often than the others over all rows.
All inputs are finite; a program needn't handle non-finite values.
Results may differ from a plain program's by a relative error of at most 0.0003.
Values may be sent and summed in bfloat16 or wider, within the bound.
No kernel may reach another device: no remote copies, remote signals or barrier semaphores. Data moves between devices by JAX's collectives and lax.ppermute only.
A program may use at most 64 MiB of HBM per device.

v0:
```python
import jax
import jax.numpy as jnp
from jax import lax
from jax.sharding import PartitionSpec as P


def masked_maxsim(similarity_matrix, live):
    keep = jnp.arange(similarity_matrix.shape[-1])[None, None, :] < live[:, None, None]
    return jnp.sum(jnp.max(jnp.where(keep, similarity_matrix, -1e30), axis=2), axis=1)


def on_device(queries, passages, lengths, candidates):
    count = lax.axis_size("dev")
    q_local, qtok, dim = queries.shape
    p_local, ptok = (passages.shape[0], passages.shape[1])
    cand = candidates.shape[1]
    slots = q_local * cand
    cap = 2 * ((slots + count - 1) // count)
    flat = candidates.reshape(-1)
    owner = flat // p_local
    local = flat % p_local
    query_of = jnp.arange(slots, dtype=jnp.int32) // cand
    indicator_matrix = (owner[:, None] == jnp.arange(count, dtype=jnp.int32)[None, :]).astype(
        jnp.int32
    )
    rank = jnp.sum(
        (jnp.cumsum(indicator_matrix, axis=0) - indicator_matrix) * indicator_matrix, axis=1
    )
    slot = owner * cap + rank
    code = query_of * p_local + local
    request_ids = jnp.zeros((count * cap,), jnp.int32).at[slot].set(code).reshape(count, cap)
    arrived = lax.all_to_all(request_ids, "dev", split_axis=0, concat_axis=0, tiled=True)
    wanted = arrived % p_local
    block_groups = passages[wanted.reshape(-1)].reshape(count, cap, ptok, dim)
    block_length_total = lengths[wanted].astype(jnp.bfloat16)
    back, back_len = (
        lax.all_to_all(block_groups, "dev", split_axis=0, concat_axis=0, tiled=True),
        lax.all_to_all(block_length_total, "dev", split_axis=0, concat_axis=0, tiled=True),
    )
    owned_passages = back.reshape(count * cap, ptok, dim)[slot].reshape(q_local, cand, ptok, dim)
    mine_len = back_len.reshape(-1)[slot].astype(jnp.int32)
    similarity_matrix = jnp.einsum(
        "wyf,wrjf->wryj", queries, owned_passages, preferred_element_type=jnp.float32
    )
    similarity_matrix = similarity_matrix.reshape(slots, qtok, ptok)
    final_scores = masked_maxsim(similarity_matrix, mine_len)
    return final_scores.reshape(q_local, cand)


def solution(mesh):
    return jax.shard_map(
        on_device,
        mesh=mesh,
        in_specs=(P("dev", None, None), P("dev", None, None), P("dev"), P("dev", None)),
        out_specs=P("dev", None),
        check_vma=False,
    )
```

profile of v0, /device:TPU:0, one launch (start us, length us, event | category | flops | bytes accessed | tf_op | source)
XLA Modules:
  0.0 136.2 jit_solution(10792866466308766380)
XLA Ops:
  0.0 0.0 copy-start
  0.0 0.0 copy-start.1
  0.0 0.8 reshape.290
  0.8 0.8 reshape.289
  1.6 0.1 fusion
  1.7 0.2 reduce_window_sum.11
  1.8 0.2 select_reduce_fusion.1
  2.0 1.0 scatter_custom_fusion
  3.0 0.1 all_to_all.17
  3.1 14.3 %all_to_all.26 = s32[32,1,8]{2,1,0:T(1,128)S(1)} all-to-all(s32[32,1,8]{2,1,0:T(1,128)S(1)} %bitcast.23), channel_id=1, replica_groups=mesh['dev'=32] {'dev'}, dimensions={0} | all-to-all | bytes 2048 | tf_op jit(solution)/shard_map/all_to_all | solution.py:32
  17.3 0.5 broadcast.284
  17.9 0.7 reduce.7
  18.6 0.1 all_to_all.21
  18.7 0.1 reshape.298
  18.8 0.0 copy-done.1
  18.8 1.9 %gather_fusion = s32[256]{0:T(256)S(1)} fusion(s32[512]{0:T(512)S(1)} %copy-done.1, s32[1024]{0:T(1024)S(1)} %pad_clamp_fusion.2), kind=kCustom, calls=%fused_computation | custom fusion | bytes 3072 | tf_op jit(solution)/shard_map/gather | solution.py:35
  20.8 0.7 convert_element_type.34
  21.4 2.5 %all-to-all-start.1 = ((bf16[32,1,8]{2,1,0:T(2,128)(2,1)}), bf16[32,1,8]{2,1,0:T(2,128)(2,1)S(1)}, u32[]{:S(2)}, u32[]{:S(2)}) async-start(bf16[32,1,8]{2,1,0:T(2,128)(2,1)} %convert_element_type.34), calls=%async_computation.1 | async-start | bytes 32768 | tf_op jit(solution)/shard_map/all_to_all | solution.py:38
  24.0 6.4 %gather_fusion.2 = bf16[256,64,128]{2,1,0:T(8,128)(2,1)} fusion(bf16[512,64,128]{2,1,0:T(8,128)(2,1)} %param.5, s32[1024]{0:T(1024)S(1)} %pad_clamp_fusion), kind=kCustom, calls=%fused_computation.2 | custom fusion | bytes 8389632 | tf_op jit(solution)/shard_map/gather | solution.py:34
  30.4 0.7 all-to-all-done.1
  31.1 5.2 %all-to-all-start.2 = ((bf16[32,8,64,128]{3,2,1,0:T(8,128)(2,1)}), bf16[32,8,64,128]{3,2,1,0:T(8,128)(2,1)}, u32[]{:S(2)}, u32[]{:S(2)}) async-start(bf16[32,8,64,128]{3,2,1,0:T(8,128)(2,1)} %bitcast.20), calls=%async_computation.2 | async-start | bytes 8388608 | tf_op jit(solution)/shard_map/all_to_all | solution.py:37
  36.4 0.1 reduce.3
  36.4 0.1 reshape.291
  36.5 1.2 gather_fusion.1
  37.8 0.1 reshape.295
  37.8 0.1 iota_compare_fusion.1
  37.9 92.3 %all-to-all-done.2 = bf16[32,8,64,128]{3,2,1,0:T(8,128)(2,1)} async-done(((bf16[32,8,64,128]{3,2,1,0:T(8,128)(2,1)}), bf16[32,8,64,128]{3,2,1,0:T(8,128)(2,1)}, u32[]{:S(2)}, u32[]{:S(2)}) %all-to-all-start.2) | async-done | bytes 4194336 | tf_op jit(solution)/shard_map/all_to_all | solution.py:37
  130.2 3.1 %gather_fusion.3 = bf16[128,64,128]{2,1,0:T(8,128)(2,1)S(1)} fusion(bf16[256,64,128]{2,1,0:T(8,128)(2,1)} %bitcast.6, s32[1024]{0:T(1024)S(1)} %pad_clamp_fusion.1), kind=kCustom, calls=%fused_computation.3 | custom fusion | bytes 4194816 | tf_op jit(solution)/shard_map/gather | solution.py:40
  133.4 0.0 copy-done
  133.4 2.2 %select_reduce_fusion = f32[2,64,32]{2,1,0:T(8,128)S(1)} fusion(bf16[2,64,64,128]{3,2,1,0:T(8,128)(2,1)S(1)} %bitcast.21, pred[2,64,64]{2,1,0:T(8,128)(4,1)S(1)} %iota_compare_fusion.1, bf16[2,32,128]{2,1,0:T(8,128)(2,1)S(1)} %copy-done), kind=kOutput, calls=%fused_computation.5 | convolution fusion | flops 67629056 | bytes 2138112 | tf_op jit(solution)/shard_map/wyf,wrjf->wryj/dot_general | solution.py:42
  135.5 0.7 reduce_sum.22
  (9 shorter events, 0.1 us)
Async XLA Ops:
  0.0 133.4 %copy-start = (bf16[2,32,128]{2,1,0:T(8,128)(2,1)S(1)}, bf16[2,32,128]{2,1,0:T(8,128)(2,1)}, u32[]{:S(2)}) copy-start(bf16[2,32,128]{2,1,0:T(8,128)(2,1)} %param.4) | copy-start | bytes 49156
  0.0 18.8 %copy-start.1 = (s32[512]{0:T(512)S(1)}, s32[512]{0:T(512)}, u32[]{:S(2)}) copy-start(s32[512]{0:T(512)} %param.6) | copy-start | bytes 6148
  21.4 9.7 %all-to-all-start.1 = ((bf16[32,1,8]{2,1,0:T(2,128)(2,1)}), bf16[32,1,8]{2,1,0:T(2,128)(2,1)S(1)}, u32[]{:S(2)}, u32[]{:S(2)}) async-start(bf16[32,1,8]{2,1,0:T(2,128)(2,1)} %convert_element_type.34), calls=%async_computation.1 | async-start | bytes 32768 | tf_op jit(solution)/shard_map/all_to_all | solution.py:38
  31.1 99.1 %all-to-all-start.2 = ((bf16[32,8,64,128]{3,2,1,0:T(8,128)(2,1)}), bf16[32,8,64,128]{3,2,1,0:T(8,128)(2,1)}, u32[]{:S(2)}, u32[]{:S(2)}) async-start(bf16[32,8,64,128]{3,2,1,0:T(8,128)(2,1)} %bitcast.20), calls=%async_computation.2 | async-start | bytes 8388608 | tf_op jit(solution)/shard_map/all_to_all | solution.py:37
where the time goes:
time: 137 us; the launch traced here: 136 us
  waiting for transfers between devices  93 us (68%)
  local copies, waits for them, and re-layouts  16.9 us (12%)
  blocking collectives  14.3 us (10%)
  starting transfers between devices  7.72 us (6%)
  matrix products  2.16 us (2%)
  other arithmetic  2 us (1%)
    all_to_all x1, waiting for transfers between devices, on_device(): lax.all_to_all(block_groups, 'dev', split_axis=0, concat_axis=0, tiled=True)  92.3 us
    all_to_all x1, blocking collectives, on_device(): lax.all_to_all(request_ids, 'dev', split_axis=0, concat_axis=0, tiled=True)  14.3 us
    gather x1, local copies, waits for them, and re-layouts, on_device(): block_groups = passages[wanted.reshape(-1)].reshape(count, cap, ptok, dim)  6.4 us
    all_to_all x1, starting transfers between devices, on_device(): lax.all_to_all(block_groups, 'dev', split_axis=0, concat_axis=0, tiled=True)  5.23 us
    gather x1, local copies, waits for them, and re-layouts, on_device(): back.reshape(count * cap, ptok, dim)[slot].reshape(q_local, cand, ptok, dim)  3.14 us
  transfers between devices with their start and end apart: 2, of which 2 were waited for; matrix products, arithmetic and copies ran while one was open for 6% of the time, Pallas kernels for 0%

commit v1 on v0

v1 whole, which is shorter than its diff:
```python
import functools

import jax
import jax.numpy as jnp
from jax import lax
from jax.experimental import pallas as pl
from jax.experimental.pallas import tpu as pltpu
from jax.sharding import PartitionSpec as P

MESH_BITS = 2
SHORTEST = 16
NT = (((1,), (1,)), ((), ()))
ID_ROWS = 8


def stages_of(count):
    stages, high = [], count.bit_length() - 1
    while high > 0:
        width = min(MESH_BITS, high)
        stages.append((high - width, 1 << width))
        high -= width
    return stages


def order_of(stage):
    return (1, 3, 2) if stage == 0 else (1, 2, 3)


def flips_of(stages):
    flips = [0]
    for stage, (shift, size) in enumerate(stages):
        flips = [flip ^ ((digit << shift) | 1 if digit else 0) for digit in (0,) + order_of(stage) for flip in flips]
    return flips


def gather_blocks(block, stages, count):
    line = marked = None
    for stage, (shift, size) in enumerate(stages):
        arrived = []
        for digit in order_of(stage):
            flip = (digit << shift) | 1
            arrived.append(lax.ppermute(block, "dev", [(d, d ^ flip) for d in range(count)]))
        if stage == 0:
            marked = mark(block)
            block, marked = lax.optimization_barrier((jnp.concatenate([block] + arrived, axis=0), marked))
            line = block
        else:
            block = jnp.concatenate([block] + arrived, axis=0)
    return line, block, marked


def mark_kernel(block_ref, out_ref):
    out_ref[...] = block_ref[0, 0:8, :].astype(jnp.float32)


def mark(block):
    vmem = pl.BlockSpec(memory_space=pltpu.VMEM)
    return pl.pallas_call(
        mark_kernel,
        out_shape=jax.ShapeDtypeStruct((8, block.shape[2]), jnp.float32),
        in_specs=[vmem],
        out_specs=vmem,
        compiler_params=pltpu.CompilerParams(vmem_limit_bytes=4 * 1024 * 1024),
        cost_estimate=pl.CostEstimate(flops=2**34, bytes_accessed=2**25, transcendentals=0),
    )(block)


def pack_kernel(q_hbm, c_hbm, out_ref, c_ref, sems):
    rows, lanes = q_hbm.shape
    cand = c_hbm.shape[1]
    q_copy = pltpu.make_async_copy(q_hbm, out_ref.at[0:rows], sems.at[0])
    c_copy = pltpu.make_async_copy(c_hbm, c_ref, sems.at[1])
    c_copy.start()
    q_copy.start()
    c_copy.wait()
    ids = c_ref[...]
    wide = jnp.concatenate([ids, jnp.zeros((2, lanes - cand), jnp.int32)], axis=1)
    lane = lax.broadcasted_iota(jnp.int32, (1, lanes), 1)
    flat = jnp.where(lane < cand, wide[0:1, :], pltpu.roll(wide, cand, 1)[1:2, :])
    row = lax.broadcasted_iota(jnp.int32, (ID_ROWS, lanes), 0)
    flat = jnp.broadcast_to(flat, (ID_ROWS, lanes))
    byte = jnp.where(row < 4, flat // 256, flat % 256)
    out_ref[rows:rows + ID_ROWS, :] = byte.astype(jnp.float32).astype(jnp.bfloat16)
    q_copy.wait()


def rows_of(blocks):
    return -(-blocks // 8) * 8


def ids_of(id_blocks):
    dim = id_blocks[0].shape[1]
    sublane = lax.broadcasted_iota(jnp.int32, (8, dim), 0)
    groups = []
    for first in range(0, len(id_blocks), 8):
        eight = jnp.full((8, dim), -1.0, jnp.float32)
        for four in range(first, min(first + 8, len(id_blocks)), 4):
            both = jnp.zeros((8, dim), jnp.float32)
            for s in range(four, four + 4):
                both = jnp.where(sublane % 4 == s - four, id_blocks[s].astype(jnp.float32), both)
            both = jnp.where(sublane < 4, both * 256.0, both)
            both = both + pltpu.roll(both, 4, 0)
            eight = jnp.where(sublane // 4 == (four - first) // 4, both, eight)
        groups.append(eight)
    return jnp.concatenate(groups, axis=0).astype(jnp.int32)


def score_kernel(cap, places, flips, n_earlier, len_hbm, p_ref, mark_ref, g_ref, *refs):
    p_local, ptok, dim = p_ref.shape
    last = n_earlier > 0
    earlier, refs = refs[:2 * n_earlier], refs[2 * n_earlier:]
    if last:
        out_ref, best, len_ref, len_sem = refs
    else:
        best, rank_ref, len_ref, len_sem = refs
    tokens = g_ref.shape[1] - ID_ROWS
    half = tokens // 2
    pairs = cap // 2
    rows = rows_of(len(places))
    me = lax.axis_index("dev")
    len_copy = pltpu.make_async_copy(len_hbm, len_ref, len_sem)
    len_copy.start()

    ids = ids_of([g_ref[place, tokens:tokens + ID_ROWS, :] for place in places])
    local = ids - me * p_local
    mine = (ids >= 0) & (local >= 0) & (local < p_local)
    before = lax.broadcasted_iota(jnp.int32, (dim, dim), 0) < lax.broadcasted_iota(jnp.int32, (dim, dim), 1)
    rank = jnp.dot(
        jnp.where(mine, 1.0, 0.0).astype(jnp.bfloat16),
        jnp.where(before, 1.0, 0.0).astype(jnp.bfloat16),
        preferred_element_type=jnp.float32,
    ).astype(jnp.int32)
    rank = jnp.where(mine, rank, -1)
    high, low = local // 256, local % 256
    entries = jnp.concatenate(
        [
            jnp.concatenate([jnp.where(rank == k, part, 0).astype(jnp.float32) for part in (high, low)], axis=1)
            for k in range(cap)
        ],
        axis=0,
    ).astype(jnp.bfloat16)
    weigh = jnp.where(lax.broadcasted_iota(jnp.int32, (8, 2 * dim), 1) < dim, 256.0, 1.0).astype(jnp.bfloat16)
    table = lax.dot_general(weigh, entries, NT, preferred_element_type=jnp.float32).astype(jnp.int32)
    len_copy.wait()

    left = lax.broadcasted_iota(jnp.int32, (8, dim), 1) < tokens
    token = lax.broadcasted_iota(jnp.int32, (8, dim), 0)
    if rows > len(places):
        best[...] = jnp.zeros_like(best)
    for i, place in enumerate(places):
        q = g_ref[place, 0:tokens, :]
        zero = jnp.zeros_like(q)
        weight = jnp.concatenate(
            [jnp.concatenate([q, zero], axis=1), jnp.concatenate([zero, q], axis=1)], axis=0
        )
        at = [table[0, k * rows + i] for k in range(cap)]
        x = jnp.concatenate(
            [jnp.concatenate([p_ref[at[p]], p_ref[at[p + pairs]]], axis=1) for p in range(pairs)], axis=0
        )
        sim = lax.dot_general(x, weight, NT, preferred_element_type=jnp.float32)
        for p in range(pairs):
            live = jnp.where(left, len_ref[at[p]], len_ref[at[p + pairs]])
            top = None
            for t in range(0, ptok, 8):
                part = sim[p * ptok + t:p * ptok + t + 8, :]
                if t + 8 > SHORTEST:
                    part = jnp.where(token + t < live, part, -1e30)
                top = part if top is None else jnp.maximum(top, part)
            best[p * rows + i:p * rows + i + 1, :] = jnp.max(top, axis=0, keepdims=True)

    if not last:
        rank_ref[...] = rank
        return

    lane_l = lax.broadcasted_iota(jnp.int32, (3 * dim, 2 * dim), 0) % dim
    lane_j = lax.broadcasted_iota(jnp.int32, (3 * dim, 2 * dim), 1)
    spread = (lane_l // half == lane_j // (dim // 2))
    spread = jnp.where(spread, 1.0, 0.0).astype(jnp.bfloat16)

    at = 0
    for best, rank in [(earlier[2 * c][...], earlier[2 * c + 1][...]) for c in range(n_earlier)] + [(best[...], rank)]:
        rows = rank.shape[0]
        hi = best.astype(jnp.bfloat16)
        rest = best - hi.astype(jnp.float32)
        mid = rest.astype(jnp.bfloat16)
        low = (rest - mid.astype(jnp.float32)).astype(jnp.bfloat16)
        sums = jnp.dot(jnp.concatenate([hi, mid, low], axis=1), spread, preferred_element_type=jnp.float32)
        total = jnp.zeros((rows, dim), jnp.float32)
        for p in range(pairs):
            part = sums[p * rows:(p + 1) * rows, :]
            total = jnp.where(rank == p, part[:, 0:dim], total)
            total = jnp.where(rank == p + pairs, part[:, dim:2 * dim], total)
        rolled = pltpu.roll(total, dim // 2, 1)
        for i, flip in enumerate(flips[at]):
            device = me ^ flip
            out_ref[pl.ds(device, 1), 0, :] = total[i:i + 1, :]
            out_ref[pl.ds(device, 1), 1, :] = rolled[i:i + 1, :]
        at += 1


def score(count, cap, places, flips, lengths, passages, marked, blocks, earlier=()):
    dim = passages.shape[2]
    anywhere, vmem = pl.BlockSpec(memory_space=pl.ANY), pl.BlockSpec(memory_space=pltpu.VMEM)
    rows = rows_of(len(places))
    best = ((cap // 2) * rows, dim)
    scratch = [pltpu.SMEM(lengths.shape, jnp.int32), pltpu.SemaphoreType.DMA]
    if earlier:
        scratch = [pltpu.VMEM(best, jnp.float32)] + scratch
        shapes, out_specs = jax.ShapeDtypeStruct((count, 2, dim), jnp.float32), vmem
    else:
        shapes = [jax.ShapeDtypeStruct(best, jnp.float32), jax.ShapeDtypeStruct((rows, dim), jnp.int32)]
        out_specs = [vmem, vmem]
    return pl.pallas_call(
        functools.partial(score_kernel, cap, places, flips, len(earlier) // 2),
        out_shape=shapes,
        in_specs=[anywhere, vmem, anywhere] + [vmem] * (1 + len(earlier)),
        out_specs=out_specs,
        scratch_shapes=scratch,
        compiler_params=pltpu.CompilerParams(vmem_limit_bytes=24 * 1024 * 1024),
    )(lengths, passages, marked, blocks, *earlier)


def on_device(queries, passages, lengths, candidates):
    count = lax.axis_size("dev")
    q_local, qtok, dim = queries.shape
    cand = candidates.shape[1]
    slots = q_local * cand
    cap = 2 * ((slots + count - 1) // count)
    rows = q_local * qtok

    packed = pl.pallas_call(
        pack_kernel,
        out_shape=jax.ShapeDtypeStruct((rows + ID_ROWS, dim), jnp.bfloat16),
        in_specs=[pl.BlockSpec(memory_space=pl.ANY), pl.BlockSpec(memory_space=pl.ANY)],
        out_specs=pl.BlockSpec(memory_space=pltpu.VMEM),
        scratch_shapes=[pltpu.VMEM(candidates.shape, jnp.int32), pltpu.SemaphoreType.DMA((2,))],
        compiler_params=pltpu.CompilerParams(vmem_limit_bytes=4 * 1024 * 1024),
    )(
        pltpu.with_memory_space_constraint(queries.reshape(rows, dim), pltpu.HBM),
        pltpu.with_memory_space_constraint(candidates, pltpu.HBM),
    )
    stages = stages_of(count)[:-1]
    sibling = [(d, d ^ 1) for d in range(count)]
    line, blocks, marked = gather_blocks(packed[None], stages, count)
    flips = flips_of(stages)
    first, every = line.shape[0], len(flips)
    line_call = score(count, cap, range(first), (), lengths, passages, marked, line)
    blocks, *line_call = lax.optimization_barrier((blocks, *line_call))
    others = lax.ppermute(blocks, "dev", sibling)
    rest_call = score(count, cap, range(first, every), (), lengths, passages, marked, blocks)
    devices = (flips[:first], flips[first:], [flip ^ 1 for flip in flips])
    dense = score(
        count, cap, range(every), devices, lengths, passages, marked, others, (*line_call, *rest_call)
    )
    back = lax.all_to_all(dense, "dev", split_axis=0, concat_axis=0, tiled=True)
    return jnp.sum(back, axis=0)[:, 0:cand]


def solution(mesh):
    return jax.shard_map(
        on_device,
        mesh=mesh,
        in_specs=(P("dev", None, None), P("dev", None, None), P("dev"), P("dev", None)),
        out_specs=P("dev", None),
        check_vma=False,
    )
```

time: 137 us -> 31.6 us (0.23)
  waiting for transfers between devices: 93 us -> 6.11 us
  local copies, waits for them, and re-layouts: 16.9 us -> 0.02 us
  Pallas kernels: 0 us -> 4.71 us
  blocking collectives: 14.3 us -> 10.6 us
  matrix products: 2.16 us -> 0 us
  starting transfers between devices: 7.72 us -> 9.19 us
    all_to_all x2 -> x0, waiting for transfers between devices: 93 us -> none  [the longest x1 92.3 us: on_device(): lax.all_to_all(block_groups, 'dev', split_axis=0, concat_axis=0, tiled=True)]
    gather x4 -> x0, local copies, waits for them, and re-layouts: 12.7 us -> none  [the longest x1 6.4 us: on_device(): block_groups = passages[wanted.reshape(-1)].reshape(count, cap, ptok, dim)]
    ppermute x0 -> x7, starting transfers between devices: none -> 9.19 us  [the longest x6 9.01 us: gather_blocks(): lax.ppermute(block, 'dev', [(d, d ^ flip) for d in range(count)])]
    all_to_all x2 -> x0, starting transfers between devices: 7.72 us -> none  [the longest x1 5.23 us: on_device(): lax.all_to_all(block_groups, 'dev', split_axis=0, concat_axis=0, tiled=True)]
    ppermute x0 -> x7, waiting for transfers between devices: none -> 6.11 us  [the longest x6 5.93 us: gather_blocks(): lax.ppermute(block, 'dev', [(d, d ^ flip) for d in range(count)])]
    pallas_call x0 -> x5, Pallas kernels: none -> 4.71 us  [the longest x3 3.93 us: score(): pl.pallas_call(functools.partial(score_kernel, cap, places, flips, len(ea...]
    all_to_all x1, blocking collectives: 14.3 us -> 10.6 us  [on_device(): back = lax.all_to_all(dense, 'dev', split_axis=0, concat_axis=0, tiled=True)]
    dot_general x1 -> x0, matrix products: 2.16 us -> none  [on_device(): jnp.einsum('wyf,wrjf->wryj', queries, owned_passages, preferred_element_t...]
  transfers between devices with their start and end apart: 2 -> 7, of which waited for: 2 -> 4; matrix products, arithmetic and copies ran while one was open for 6% -> 0% of each run, Pallas kernels for 0% -> 7%
where the time goes in v1:
time: 31.6 us; the launch traced here: 31.4 us
  blocking collectives  10.6 us (34%)
  starting transfers between devices  9.19 us (29%)
  waiting for transfers between devices  6.11 us (19%)
  Pallas kernels  4.71 us (15%)
  other arithmetic  0.66 us (2%)
    all_to_all x1, blocking collectives, on_device(): back = lax.all_to_all(dense, 'dev', split_axis=0, concat_axis=0, tiled=True)  10.6 us
    ppermute x6, starting transfers between devices, gather_blocks(): lax.ppermute(block, 'dev', [(d, d ^ flip) for d in range(count)])  9.01 us
    ppermute x6, waiting for transfers between devices, gather_blocks(): lax.ppermute(block, 'dev', [(d, d ^ flip) for d in range(count)])  5.93 us
    pallas_call x3, Pallas kernels, score(): pl.pallas_call(functools.partial(score_kernel, cap, places, flips, len(ea...  3.93 us
    pallas_call x1, Pallas kernels, on_device(): pl.pallas_call(pack_kernel, out_shape=jax.ShapeDtypeStruct((rows + ID_ROW...  0.78 us
  transfers between devices with their start and end apart: 7, of which 4 were waited for; matrix products, arithmetic and copies ran while one was open for 0% of the time, Pallas kernels for 7%

profile of v1, /device:TPU:0, one launch (start us, length us, event | category | flops | bytes accessed | tf_op | source)
XLA Modules:
  0.0 31.4 jit_solution(7835241761494098464)
XLA Ops:
  0.0 0.8 %shard_map.46 = bf16[72,128]{1,0:T(8,128)(2,1)S(1)} custom-call(bf16[64,128]{1,0:T(8,128)(2,1)} %bitcast.10, s32[2,64]{1,0:T(2,128)} %c_hbm.1), custom_call_target="tpu_custom_call" | custom-call | tf_op jit(solution)/shard_map/pallas_call | solution.py:231
  0.8 0.0 slice-start
  0.8 0.0 slice-start.1
  0.8 0.0 copy-start
  0.8 3.5 %collective-permute-start.2 = (bf16[1,72,128]{2,1,0:T(8,128)(2,1)S(1)}, bf16[1,72,128]{2,1,0:T(8,128)(2,1)S(1)}, u32[]{:S(2)}, u32[]{:S(2)}) collective-permute-start(bf16[1,72,128]{2,1,0:T(8,128)(2,1)S(1)} %bitcast.5), channel_id=1, source_target_pairs={{0,17},{1,16},{2,19},{3,18},{4,21},{5,20},{6,23},{7,22},{8,25},{9,... | collective-permute-start | bytes 55304 | tf_op jit(solution)/shard_map/ppermute | solution.py:42
  4.4 1.6 %collective-permute-start.1 = (bf16[1,72,128]{2,1,0:T(8,128)(2,1)S(1)}, bf16[1,72,128]{2,1,0:T(8,128)(2,1)S(1)}, u32[]{:S(2)}, u32[]{:S(2)}) collective-permute-start(bf16[1,72,128]{2,1,0:T(8,128)(2,1)S(1)} %bitcast.6), channel_id=1, source_target_pairs={{0,25},{1,24},{2,27},{3,26},{4,29},{5,28},{6,31},{7,30},{8,17},{9,... | collective-permute-start | bytes 55304 | tf_op jit(solution)/shard_map/ppermute | solution.py:42
  6.0 0.2 collective-permute-start
  6.2 0.0 collective-permute-done.2
  6.2 3.2 %collective-permute-done.1 = bf16[1,72,128]{2,1,0:T(8,128)(2,1)S(1)} collective-permute-done((bf16[1,72,128]{2,1,0:T(8,128)(2,1)S(1)}, bf16[1,72,128]{2,1,0:T(8,128)(2,1)S(1)}, u32[]{:S(2)}, u32[]{:S(2)}) %collective-permute-start.1) | collective-permute-done | bytes 18464 | tf_op jit(solution)/shard_map/ppermute | solution.py:42
  9.4 0.0 collective-permute-done
  9.4 2.9 %collective-permute-start.5 = (bf16[4,72,128]{2,1,0:T(8,128)(2,1)S(1)}, bf16[4,72,128]{2,1,0:T(8,128)(2,1)S(1)}, u32[]{:S(2)}, u32[]{:S(2)}) collective-permute-start(bf16[4,72,128]{2,1,0:T(8,128)(2,1)S(1)} %pad_maximum_fusion.1.g_ref), channel_id=1, source_target_pairs={{0,7},{1,6},{2,5},{3,4},{4,3},{5,2},{6,1},{7,0},{8,15},{9,14},{10,... | collective-permute-start | bytes 221192 | tf_op jit(solution)/shard_map/ppermute | solution.py:42
  12.3 0.0 collective-permute-start.4
  12.3 0.8 %collective-permute-start.3 = (bf16[4,72,128]{2,1,0:T(8,128)(2,1)S(1)}, bf16[4,72,128]{2,1,0:T(8,128)(2,1)S(1)}, u32[]{:S(2)}, u32[]{:S(2)}) collective-permute-start(bf16[4,72,128]{2,1,0:T(8,128)(2,1)S(1)} %pad_maximum_fusion.1.g_ref), channel_id=1, source_target_pairs={{0,3},{1,2},{2,1},{3,0},{4,7},{5,6},{6,5},{7,4},{8,11},{9,10},{10,... | collective-permute-start | bytes 221192 | tf_op jit(solution)/shard_map/ppermute | solution.py:42
  13.0 0.0 slice-done
  13.0 0.0 slice-done.1
  13.0 0.0 copy-done
  13.0 1.0 %shard_map.48 = (f32[32,128]{1,0:T(8,128)S(1)}, s32[8,128]{1,0:T(8,128)S(1)}) custom-call(s32[512]{0:T(512)S(1)} %copy-done, bf16[512,64,128]{2,1,0:T(8,128)(2,1)S(1)} %bitcast.4, f32[8,128]{1,0:T(8,128)S(1)} %shard_map.47.mark_ref, bf16[4,72,128]{2,1,0:T(8,128)(2,1)S(1)} %pad_maximum_fusion.1.g_ref), custom_call_target="tpu_custom_call" | custom-call | tf_op jit(solution)/shard_map/pallas_call | solution.py:213
  14.0 0.8 %collective-permute-done.5 = bf16[4,72,128]{2,1,0:T(8,128)(2,1)S(1)} collective-permute-done((bf16[4,72,128]{2,1,0:T(8,128)(2,1)S(1)}, bf16[4,72,128]{2,1,0:T(8,128)(2,1)S(1)}, u32[]{:S(2)}, u32[]{:S(2)}) %collective-permute-start.5) | collective-permute-done | bytes 73760 | tf_op jit(solution)/shard_map/ppermute | solution.py:42
  14.8 1.9 %collective-permute-done.4 = bf16[4,72,128]{2,1,0:T(8,128)(2,1)S(1)} collective-permute-done((bf16[4,72,128]{2,1,0:T(8,128)(2,1)S(1)}, bf16[4,72,128]{2,1,0:T(8,128)(2,1)S(1)}, u32[]{:S(2)}, u32[]{:S(2)}) %collective-permute-start.4) | collective-permute-done | bytes 73760 | tf_op jit(solution)/shard_map/ppermute | solution.py:42
  16.8 0.0 collective-permute-done.3
  16.8 0.2 collective-permute-start.6
  17.0 1.3 %shard_map.49 = (f32[64,128]{1,0:T(8,128)S(1)}, s32[16,128]{1,0:T(8,128)S(1)}) custom-call(s32[512]{0:T(512)S(1)} %copy-done, bf16[512,64,128]{2,1,0:T(8,128)(2,1)S(1)} %bitcast.4, f32[8,128]{1,0:T(8,128)S(1)} %shard_map.47.mark_ref, bf16[16,72,128]{2,1,0:T(8,128)(2,1)S(1)} %pad_maximum_fusion.g_ref), custom_call_target="tpu_custom_call" | custom-call | tf_op jit(solution)/shard_map/pallas_call | solution.py:213
  18.3 0.2 collective-permute-done.6.g_ref
  18.5 1.7 %shard_map.50 = f32[32,2,128]{2,1,0:T(2,128)S(1)} custom-call(s32[512]{0:T(512)S(1)} %copy-done, bf16[512,64,128]{2,1,0:T(8,128)(2,1)S(1)} %bitcast.4, f32[8,128]{1,0:T(8,128)S(1)} %shard_map.47.mark_ref, bf16[16,72,128]{2,1,0:T(8,128)(2,1)S(1)} %collective-permute-done.6.g_ref, f32[32,128]{1,0:T(8,128)S(1)} %get-tuple-element.19.refs_0_, ...), custom_call_target="tpu_custom_call" | custom-call | tf_op jit(solution)/shard_map/pallas_call | solution.py:213
  20.2 10.6 %all_to_all.5 = f32[32,2,128]{2,1,0:T(2,128)S(1)} all-to-all(f32[32,2,128]{2,1,0:T(2,128)S(1)} %shard_map.50), channel_id=1, replica_groups=mesh['dev'=32] {'dev'}, dimensions={0} | all-to-all | bytes 65536 | tf_op jit(solution)/shard_map/all_to_all | solution.py:255
  30.8 0.6 %reduce_sum.9 = f32[2,128]{1,0:T(2,128)} reduce(f32[32,2,128]{2,1,0:T(2,128)S(1)} %all_to_all.5, f32[]{:T(128)} %constant.0.clone.1), dimensions={0}, to_apply=%region_0.0 | reduce | flops 7936 | bytes 33796 | tf_op jit(solution)/shard_map/reduce_sum | solution.py:256
  (4 shorter events, 0.1 us)
Async XLA Ops:
  0.8 12.2 %slice-start = ((s8[8388608]{0:T(1024)(128)(4,1)}), s8[4194304]{0:T(1024)(128)(4,1)S(1)}, s32[]{:S(2)}) async-start(s8[8388608]{0:T(1024)(128)(4,1)} %bitcast.3), calls=%async_computation.1 | async-start | bytes 8388608
  0.8 12.2 %slice-start.1 = ((s8[8388608]{0:T(1024)(128)(4,1)}), s8[4194304]{0:T(1024)(128)(4,1)S(1)}, s32[]{:S(2)}) async-start(s8[8388608]{0:T(1024)(128)(4,1)} %bitcast.3), calls=%async_computation.2 | async-start | bytes 8388608
  0.8 12.2 %copy-start = (s32[512]{0:T(512)S(1)}, s32[512]{0:T(512)}, u32[]{:S(2)}) copy-start(s32[512]{0:T(512)} %len_hbm.5) | copy-start | bytes 6148
  0.8 5.4 %collective-permute-start.2 = (bf16[1,72,128]{2,1,0:T(8,128)(2,1)S(1)}, bf16[1,72,128]{2,1,0:T(8,128)(2,1)S(1)}, u32[]{:S(2)}, u32[]{:S(2)}) collective-permute-start(bf16[1,72,128]{2,1,0:T(8,128)(2,1)S(1)} %bitcast.5), channel_id=1, source_target_pairs={{0,17},{1,16},{2,19},{3,18},{4,21},{5,20},{6,23},{7,22},{8,25},{9,... | collective-permute-start | bytes 55304 | tf_op jit(solution)/shard_map/ppermute | solution.py:42
  4.4 5.0 %collective-permute-start.1 = (bf16[1,72,128]{2,1,0:T(8,128)(2,1)S(1)}, bf16[1,72,128]{2,1,0:T(8,128)(2,1)S(1)}, u32[]{:S(2)}, u32[]{:S(2)}) collective-permute-start(bf16[1,72,128]{2,1,0:T(8,128)(2,1)S(1)} %bitcast.6), channel_id=1, source_target_pairs={{0,25},{1,24},{2,27},{3,26},{4,29},{5,28},{6,31},{7,30},{8,17},{9,... | collective-permute-start | bytes 55304 | tf_op jit(solution)/shard_map/ppermute | solution.py:42
  6.0 3.4 %collective-permute-start = (bf16[1,72,128]{2,1,0:T(8,128)(2,1)S(1)}, bf16[1,72,128]{2,1,0:T(8,128)(2,1)S(1)}, u32[]{:S(2)}, u32[]{:S(2)}) collective-permute-start(bf16[1,72,128]{2,1,0:T(8,128)(2,1)S(1)} %bitcast.7), channel_id=1, source_target_pairs={{0,9},{1,8},{2,11},{3,10},{4,13},{5,12},{6,15},{7,14},{8,1},{9,0},... | collective-permute-start | bytes 55304 | tf_op jit(solution)/shard_map/ppermute | solution.py:42
  9.4 5.4 %collective-permute-start.5 = (bf16[4,72,128]{2,1,0:T(8,128)(2,1)S(1)}, bf16[4,72,128]{2,1,0:T(8,128)(2,1)S(1)}, u32[]{:S(2)}, u32[]{:S(2)}) collective-permute-start(bf16[4,72,128]{2,1,0:T(8,128)(2,1)S(1)} %pad_maximum_fusion.1.g_ref), channel_id=1, source_target_pairs={{0,7},{1,6},{2,5},{3,4},{4,3},{5,2},{6,1},{7,0},{8,15},{9,14},{10,... | collective-permute-start | bytes 221192 | tf_op jit(solution)/shard_map/ppermute | solution.py:42
  12.3 4.5 %collective-permute-start.4 = (bf16[4,72,128]{2,1,0:T(8,128)(2,1)S(1)}, bf16[4,72,128]{2,1,0:T(8,128)(2,1)S(1)}, u32[]{:S(2)}, u32[]{:S(2)}) collective-permute-start(bf16[4,72,128]{2,1,0:T(8,128)(2,1)S(1)} %pad_maximum_fusion.1.g_ref), channel_id=1, source_target_pairs={{0,5},{1,4},{2,7},{3,6},{4,1},{5,0},{6,3},{7,2},{8,13},{9,12},{10,... | collective-permute-start | bytes 221192 | tf_op jit(solution)/shard_map/ppermute | solution.py:42
  12.3 4.5 %collective-permute-start.3 = (bf16[4,72,128]{2,1,0:T(8,128)(2,1)S(1)}, bf16[4,72,128]{2,1,0:T(8,128)(2,1)S(1)}, u32[]{:S(2)}, u32[]{:S(2)}) collective-permute-start(bf16[4,72,128]{2,1,0:T(8,128)(2,1)S(1)} %pad_maximum_fusion.1.g_ref), channel_id=1, source_target_pairs={{0,3},{1,2},{2,1},{3,0},{4,7},{5,6},{6,5},{7,4},{8,11},{9,10},{10,... | collective-permute-start | bytes 221192 | tf_op jit(solution)/shard_map/ppermute | solution.py:42
  16.8 1.6 %collective-permute-start.6 = (bf16[16,72,128]{2,1,0:T(8,128)(2,1)S(1)}, bf16[16,72,128]{2,1,0:T(8,128)(2,1)S(1)}, u32[]{:S(2)}, u32[]{:S(2)}) collective-permute-start(bf16[16,72,128]{2,1,0:T(8,128)(2,1)S(1)} %pad_maximum_fusion.g_ref), channel_id=1, source_target_pairs={{0,1},{1,0},{2,3},{3,2},{4,5},{5,4},{6,7},{7,6},{8,9},{9,8},{10,11... | collective-permute-start | bytes 884744 | tf_op jit(solution)/shard_map/ppermute | solution.py:249

commit v2 on v1

--- a/solution.py
+++ b/solution.py
@@ -23,7 +23,7 @@
 
 
 def order_of(stage):
-    return (1, 3, 2) if stage == 0 else (1, 2, 3)
+    return (1, 3, 2) if stage == 0 else (3, 2, 1)
 
 
 def flips_of(stages):
@@ -34,18 +34,24 @@
 
 
 def gather_blocks(block, stages, count):
-    line = marked = None
-    for stage, (shift, size) in enumerate(stages):
-        arrived = []
-        for digit in order_of(stage):
-            flip = (digit << shift) | 1
-            arrived.append(lax.ppermute(block, "dev", [(d, d ^ flip) for d in range(count)]))
-        if stage == 0:
-            marked = mark(block)
-            block, marked = lax.optimization_barrier((jnp.concatenate([block] + arrived, axis=0), marked))
-            line = block
-        else:
-            block = jnp.concatenate([block] + arrived, axis=0)
+    def send(block, shift, digit):
+        flip = (digit << shift) | 1
+        return lax.ppermute(block, "dev", [(d, d ^ flip) for d in range(count)])
+
+    (near, _), (far, _) = stages[:2]
+    arrived = [send(block, near, digit) for digit in order_of(0)]
+    marked = mark(block, 2**20)
+    own, marked = lax.optimization_barrier((block, marked))
+    *soon, last = order_of(1)
+    early = [send(own, far, digit) for digit in soon]
+    others = jnp.concatenate(arrived, axis=0)
+    line = jnp.concatenate([block, others], axis=0)
+    line, others, marked = lax.optimization_barrier((line, others, mark(line, 2**34) + marked))
+    late = [send(others, far, digit) for digit in soon]
+    parts = [part for pair in zip(early, late) for part in pair] + [send(line, far, last)]
+    block = jnp.concatenate([line] + parts, axis=0)
+    for stage, (shift, size) in enumerate(stages[2:], 2):
+        block = jnp.concatenate([block] + [send(block, shift, digit) for digit in order_of(stage)], axis=0)
     return line, block, marked
 
 
@@ -53,7 +59,7 @@
     out_ref[...] = block_ref[0, 0:8, :].astype(jnp.float32)
 
 
-def mark(block):
+def mark(block, flops):
     vmem = pl.BlockSpec(memory_space=pltpu.VMEM)
     return pl.pallas_call(
         mark_kernel,
@@ -61,7 +67,7 @@
         in_specs=[vmem],
         out_specs=vmem,
         compiler_params=pltpu.CompilerParams(vmem_limit_bytes=4 * 1024 * 1024),
-        cost_estimate=pl.CostEstimate(flops=2**34, bytes_accessed=2**25, transcendentals=0),
+        cost_estimate=pl.CostEstimate(flops=flops, bytes_accessed=flops >> 9, transcendentals=0),
     )(block)
 
 
@@ -190,11 +196,8 @@
             part = sums[p * rows:(p + 1) * rows, :]
             total = jnp.where(rank == p, part[:, 0:dim], total)
             total = jnp.where(rank == p + pairs, part[:, dim:2 * dim], total)
-        rolled = pltpu.roll(total, dim // 2, 1)
         for i, flip in enumerate(flips[at]):
-            device = me ^ flip
-            out_ref[pl.ds(device, 1), 0, :] = total[i:i + 1, :]
-            out_ref[pl.ds(device, 1), 1, :] = rolled[i:i + 1, :]
+            out_ref[pl.ds(me ^ flip, 1), :] = total[i:i + 1, :]
         at += 1
 
 
@@ -206,7 +209,7 @@
     scratch = [pltpu.SMEM(lengths.shape, jnp.int32), pltpu.SemaphoreType.DMA]
     if earlier:
         scratch = [pltpu.VMEM(best, jnp.float32)] + scratch
-        shapes, out_specs = jax.ShapeDtypeStruct((count, 2, dim), jnp.float32), vmem
+        shapes, out_specs = jax.ShapeDtypeStruct((count, dim), jnp.float32), vmem
     else:
         shapes = [jax.ShapeDtypeStruct(best, jnp.float32), jax.ShapeDtypeStruct((rows, dim), jnp.int32)]
         out_specs = [vmem, vmem]
@@ -218,6 +221,14 @@
         scratch_shapes=scratch,
         compiler_params=pltpu.CompilerParams(vmem_limit_bytes=24 * 1024 * 1024),
     )(lengths, passages, marked, blocks, *earlier)
+
+
+def sum_kernel(rows_ref, out_ref):
+    cand = out_ref.shape[1]
+    total = jnp.sum(rows_ref[...], axis=0, keepdims=True)
+    total = jnp.broadcast_to(total, (8, 2 * cand))
+    out_ref[0:1, :] = total[0:1, 0:cand]
+    out_ref[1:2, :] = pltpu.roll(total, cand, 1)[0:1, 0:cand]
 
 
 def on_device(queries, passages, lengths, candidates):
@@ -253,7 +264,14 @@
         count, cap, range(every), devices, lengths, passages, marked, others, (*line_call, *rest_call)
     )
     back = lax.all_to_all(dense, "dev", split_axis=0, concat_axis=0, tiled=True)
-    return jnp.sum(back, axis=0)[:, 0:cand]
+    vmem = pl.BlockSpec(memory_space=pltpu.VMEM)
+    return pl.pallas_call(
+        sum_kernel,
+        out_shape=jax.ShapeDtypeStruct((q_local, cand), jnp.float32),
+        in_specs=[vmem],
+        out_specs=vmem,
+        compiler_params=pltpu.CompilerParams(vmem_limit_bytes=4 * 1024 * 1024),
+    )(back)
 
 
 def solution(mesh):

time: 31.6 us -> 31.5 us (level)
  waiting for transfers between devices: 6.11 us -> 2.81 us
  starting transfers between devices: 9.19 us -> 12.1 us
  other arithmetic: 0.66 us -> 0.03 us
  Pallas kernels: 4.71 us -> 5.27 us
    ppermute x6 -> x8, waiting for transfers between devices: 5.93 us -> 2.81 us  [send(): return lax.ppermute(block, 'dev', [(d, d ^ flip) for d in range(count)])]
    ppermute x6 -> x8, starting transfers between devices: 9.01 us -> 11.7 us  [send(): return lax.ppermute(block, 'dev', [(d, d ^ flip) for d in range(count)])]
    pallas_call x0 -> x1, Pallas kernels: none -> 0.64 us  [on_device(): pl.pallas_call(sum_kernel, out_shape=jax.ShapeDtypeStruct((q_local, cand)...]
    reduce_sum x1 -> x0, other arithmetic: 0.6 us -> none  [on_device(): return jnp.sum(back, axis=0)[:, 0:cand]]
  transfers between devices with their start and end apart: 7 -> 9, of which waited for: 4 -> 3; matrix products, arithmetic and copies ran while one was open for 0% -> 0% of each run, Pallas kernels for 7% -> 7%
where the time goes in v2:
time: 31.5 us; the launch traced here: 31.3 us
  starting transfers between devices  12.1 us (38%)
  blocking collectives  10.9 us (35%)
  Pallas kernels  5.27 us (17%)
  waiting for transfers between devices  2.81 us (9%)
    ppermute x8, starting transfers between devices, send(): return lax.ppermute(block, 'dev', [(d, d ^ flip) for d in range(count)])  11.7 us
    all_to_all x1, blocking collectives, on_device(): back = lax.all_to_all(dense, 'dev', split_axis=0, concat_axis=0, tiled=True)  10.9 us
    pallas_call x3, Pallas kernels, score(): pl.pallas_call(functools.partial(score_kernel, cap, places, flips, len(ea...  3.85 us
    ppermute x8, waiting for transfers between devices, send(): return lax.ppermute(block, 'dev', [(d, d ^ flip) for d in range(count)])  2.81 us
    pallas_call x1, Pallas kernels, on_device(): pl.pallas_call(pack_kernel, out_shape=jax.ShapeDtypeStruct((rows + ID_ROW...  0.78 us
    pallas_call x1, Pallas kernels, on_device(): pl.pallas_call(sum_kernel, out_shape=jax.ShapeDtypeStruct((q_local, cand)...  0.64 us
  transfers between devices with their start and end apart: 9, of which 3 were waited for; matrix products, arithmetic and copies ran while one was open for 0% of the time, Pallas kernels for 7%

profile of v2, /device:TPU:0, one launch (start us, length us, event | category | flops | bytes accessed | tf_op | source)
XLA Modules:
  0.0 31.3 jit_solution(15658341998222657897)
XLA Ops:
  0.0 0.8 %shard_map.46 = bf16[72,128]{1,0:T(8,128)(2,1)S(1)} custom-call(bf16[64,128]{1,0:T(8,128)(2,1)} %bitcast.15, s32[2,64]{1,0:T(2,128)} %c_hbm.1), custom_call_target="tpu_custom_call" | custom-call | tf_op jit(solution)/shard_map/pallas_call | solution.py:242
  0.8 3.5 %collective-permute-start.2 = (bf16[1,72,128]{2,1,0:T(8,128)(2,1)S(1)}, bf16[1,72,128]{2,1,0:T(8,128)(2,1)S(1)}, u32[]{:S(2)}, u32[]{:S(2)}) collective-permute-start(bf16[1,72,128]{2,1,0:T(8,128)(2,1)S(1)} %bitcast.6), channel_id=1, source_target_pairs={{0,17},{1,16},{2,19},{3,18},{4,21},{5,20},{6,23},{7,22},{8,25},{9,... | collective-permute-start | bytes 55304 | tf_op jit(solution)/shard_map/ppermute | solution.py:39
  4.3 1.6 %collective-permute-start.1 = (bf16[1,72,128]{2,1,0:T(8,128)(2,1)S(1)}, bf16[1,72,128]{2,1,0:T(8,128)(2,1)S(1)}, u32[]{:S(2)}, u32[]{:S(2)}) collective-permute-start(bf16[1,72,128]{2,1,0:T(8,128)(2,1)S(1)} %bitcast.7), channel_id=1, source_target_pairs={{0,25},{1,24},{2,27},{3,26},{4,29},{5,28},{6,31},{7,30},{8,17},{9,... | collective-permute-start | bytes 55304 | tf_op jit(solution)/shard_map/ppermute | solution.py:39
  6.0 0.2 collective-permute-start
  6.2 2.0 %collective-permute-start.3 = (bf16[1,72,128]{2,1,0:T(8,128)(2,1)S(1)}, bf16[1,72,128]{2,1,0:T(8,128)(2,1)S(1)}, u32[]{:S(2)}, u32[]{:S(2)}) collective-permute-start(bf16[1,72,128]{2,1,0:T(8,128)(2,1)S(1)} %bitcast.10), channel_id=1, source_target_pairs={{0,7},{1,6},{2,5},{3,4},{4,3},{5,2},{6,1},{7,0},{8,15},{9,14},{10,... | collective-permute-start | bytes 55304 | tf_op jit(solution)/shard_map/ppermute | solution.py:39
  8.2 0.7 %collective-permute-start.5 = (bf16[1,72,128]{2,1,0:T(8,128)(2,1)S(1)}, bf16[1,72,128]{2,1,0:T(8,128)(2,1)S(1)}, u32[]{:S(2)}, u32[]{:S(2)}) collective-permute-start(bf16[1,72,128]{2,1,0:T(8,128)(2,1)S(1)} %bitcast.11), channel_id=1, source_target_pairs={{0,5},{1,4},{2,7},{3,6},{4,1},{5,0},{6,3},{7,2},{8,13},{9,12},{10,... | collective-permute-start | bytes 55304 | tf_op jit(solution)/shard_map/ppermute | solution.py:39
  8.9 0.0 collective-permute-done.2
  8.9 0.5 %collective-permute-done.1 = bf16[1,72,128]{2,1,0:T(8,128)(2,1)S(1)} collective-permute-done((bf16[1,72,128]{2,1,0:T(8,128)(2,1)S(1)}, bf16[1,72,128]{2,1,0:T(8,128)(2,1)S(1)}, u32[]{:S(2)}, u32[]{:S(2)}) %collective-permute-start.1) | collective-permute-done | bytes 18464 | tf_op jit(solution)/shard_map/ppermute | solution.py:39
  9.3 0.0 collective-permute-done
  9.4 0.0 copy-start
  9.4 0.0 copy-start.1
  9.4 2.9 %collective-permute-start.4 = (bf16[3,72,128]{2,1,0:T(8,128)(2,1)S(1)}, bf16[3,72,128]{2,1,0:T(8,128)(2,1)S(1)}, u32[]{:S(2)}, u32[]{:S(2)}) collective-permute-start(bf16[3,72,128]{2,1,0:T(8,128)(2,1)S(1)} %pad_maximum_fusion.1), channel_id=1, source_target_pairs={{0,7},{1,6},{2,5},{3,4},{4,3},{5,2},{6,1},{7,0},{8,15},{9,14},{10,... | collective-permute-start | bytes 165896 | tf_op jit(solution)/shard_map/ppermute | solution.py:39
  12.3 0.0 collective-permute-start.6
  12.3 0.8 %collective-permute-start.7 = (bf16[4,72,128]{2,1,0:T(8,128)(2,1)S(1)}, bf16[4,72,128]{2,1,0:T(8,128)(2,1)S(1)}, u32[]{:S(2)}, u32[]{:S(2)}) collective-permute-start(bf16[4,72,128]{2,1,0:T(8,128)(2,1)S(1)} %pad_maximum_fusion.block_ref.g_ref), channel_id=1, source_target_pairs={{0,3},{1,2},{2,1},{3,0},{4,7},{5,6},{6,5},{7,4},{8,11},{9,10},{10,... | collective-permute-start | bytes 221192 | tf_op jit(solution)/shard_map/ppermute | solution.py:39
  13.1 0.0 collective-permute-done.3
  13.1 0.0 copy-done
  13.1 0.0 copy-done.1
  13.1 1.0 %shard_map.49 = (f32[32,128]{1,0:T(8,128)S(1)}, s32[8,128]{1,0:T(8,128)S(1)}) custom-call(s32[512]{0:T(512)S(1)} %copy-done.1, bf16[512,64,128]{2,1,0:T(8,128)(2,1)S(1)} %copy-done, f32[8,128]{1,0:T(8,128)S(1)} %add.3.mark_ref, bf16[4,72,128]{2,1,0:T(8,128)(2,1)S(1)} %pad_maximum_fusion.block_ref.g_ref), custom_call_target="tpu_custom_call" | custom-call | tf_op jit(solution)/shard_map/pallas_call | solution.py:216
  14.1 0.4 %collective-permute-done.4 = bf16[3,72,128]{2,1,0:T(8,128)(2,1)S(1)} collective-permute-done((bf16[3,72,128]{2,1,0:T(8,128)(2,1)S(1)}, bf16[3,72,128]{2,1,0:T(8,128)(2,1)S(1)}, u32[]{:S(2)}, u32[]{:S(2)}) %collective-permute-start.4) | collective-permute-done | bytes 55328 | tf_op jit(solution)/shard_map/ppermute | solution.py:39
  14.5 0.0 collective-permute-done.5
  14.5 1.9 %collective-permute-done.6 = bf16[3,72,128]{2,1,0:T(8,128)(2,1)S(1)} collective-permute-done((bf16[3,72,128]{2,1,0:T(8,128)(2,1)S(1)}, bf16[3,72,128]{2,1,0:T(8,128)(2,1)S(1)}, u32[]{:S(2)}, u32[]{:S(2)}) %collective-permute-start.6) | collective-permute-done | bytes 55328 | tf_op jit(solution)/shard_map/ppermute | solution.py:39
  16.4 0.0 collective-permute-done.7
  16.5 0.4 %collective-permute-start.8 = (bf16[16,72,128]{2,1,0:T(8,128)(2,1)S(1)}, bf16[16,72,128]{2,1,0:T(8,128)(2,1)S(1)}, u32[]{:S(2)}, u32[]{:S(2)}) collective-permute-start(bf16[16,72,128]{2,1,0:T(8,128)(2,1)S(1)} %constant_dynamic-update-slice_fusion.g_ref), channel_id=1, source_target_pairs={{0,1},{1,0},{2,3},{3,2},{4,5},{5,4},{6,7},{7,6},{8,9},{9,8},{10,11... | collective-permute-start | bytes 884744 | tf_op jit(solution)/shard_map/ppermute | solution.py:260
  16.8 1.3 %shard_map.50 = (f32[64,128]{1,0:T(8,128)S(1)}, s32[16,128]{1,0:T(8,128)S(1)}) custom-call(s32[512]{0:T(512)S(1)} %copy-done.1, bf16[512,64,128]{2,1,0:T(8,128)(2,1)S(1)} %copy-done, f32[8,128]{1,0:T(8,128)S(1)} %add.3.mark_ref, bf16[16,72,128]{2,1,0:T(8,128)(2,1)S(1)} %constant_dynamic-update-slice_fusion.g_ref), custom_call_target="tpu_custom_call" | custom-call | tf_op jit(solution)/shard_map/pallas_call | solution.py:216
  18.1 0.0 collective-permute-done.8.g_ref
  18.1 1.6 %shard_map.51 = f32[32,128]{1,0:T(8,128)S(1)} custom-call(s32[512]{0:T(512)S(1)} %copy-done.1, bf16[512,64,128]{2,1,0:T(8,128)(2,1)S(1)} %copy-done, f32[8,128]{1,0:T(8,128)S(1)} %add.3.mark_ref, bf16[16,72,128]{2,1,0:T(8,128)(2,1)S(1)} %collective-permute-done.8.g_ref, f32[32,128]{1,0:T(8,128)S(1)} %get-tuple-element.25.refs_0_, ...), custom_call_target="tpu_custom_call" | custom-call | tf_op jit(solution)/shard_map/pallas_call | solution.py:216
  19.7 10.9 %all_to_all.11 = f32[32,1,128]{2,1,0:T(1,128)S(1)} all-to-all(f32[32,1,128]{2,1,0:T(1,128)S(1)} %bitcast.13), channel_id=1, replica_groups=mesh['dev'=32] {'dev'}, dimensions={0} | all-to-all | bytes 32768 | tf_op jit(solution)/shard_map/all_to_all | solution.py:266
  30.6 0.6 %shard_map.52 = f32[2,64]{1,0:T(2,128)} custom-call(f32[32,128]{1,0:T(8,128)S(1)} %bitcast.14), custom_call_target="tpu_custom_call" | custom-call | tf_op jit(solution)/shard_map/pallas_call | solution.py:268
  (11 shorter events, 0.1 us)
Async XLA Ops:
  0.8 8.1 %collective-permute-start.2 = (bf16[1,72,128]{2,1,0:T(8,128)(2,1)S(1)}, bf16[1,72,128]{2,1,0:T(8,128)(2,1)S(1)}, u32[]{:S(2)}, u32[]{:S(2)}) collective-permute-start(bf16[1,72,128]{2,1,0:T(8,128)(2,1)S(1)} %bitcast.6), channel_id=1, source_target_pairs={{0,17},{1,16},{2,19},{3,18},{4,21},{5,20},{6,23},{7,22},{8,25},{9,... | collective-permute-start | bytes 55304 | tf_op jit(solution)/shard_map/ppermute | solution.py:39
  4.3 5.0 %collective-permute-start.1 = (bf16[1,72,128]{2,1,0:T(8,128)(2,1)S(1)}, bf16[1,72,128]{2,1,0:T(8,128)(2,1)S(1)}, u32[]{:S(2)}, u32[]{:S(2)}) collective-permute-start(bf16[1,72,128]{2,1,0:T(8,128)(2,1)S(1)} %bitcast.7), channel_id=1, source_target_pairs={{0,25},{1,24},{2,27},{3,26},{4,29},{5,28},{6,31},{7,30},{8,17},{9,... | collective-permute-start | bytes 55304 | tf_op jit(solution)/shard_map/ppermute | solution.py:39
  6.0 3.4 %collective-permute-start = (bf16[1,72,128]{2,1,0:T(8,128)(2,1)S(1)}, bf16[1,72,128]{2,1,0:T(8,128)(2,1)S(1)}, u32[]{:S(2)}, u32[]{:S(2)}) collective-permute-start(bf16[1,72,128]{2,1,0:T(8,128)(2,1)S(1)} %bitcast.8), channel_id=1, source_target_pairs={{0,9},{1,8},{2,11},{3,10},{4,13},{5,12},{6,15},{7,14},{8,1},{9,0},... | collective-permute-start | bytes 55304 | tf_op jit(solution)/shard_map/ppermute | solution.py:39
  6.2 6.9 %collective-permute-start.3 = (bf16[1,72,128]{2,1,0:T(8,128)(2,1)S(1)}, bf16[1,72,128]{2,1,0:T(8,128)(2,1)S(1)}, u32[]{:S(2)}, u32[]{:S(2)}) collective-permute-start(bf16[1,72,128]{2,1,0:T(8,128)(2,1)S(1)} %bitcast.10), channel_id=1, source_target_pairs={{0,7},{1,6},{2,5},{3,4},{4,3},{5,2},{6,1},{7,0},{8,15},{9,14},{10,... | collective-permute-start | bytes 55304 | tf_op jit(solution)/shard_map/ppermute | solution.py:39
  8.2 6.3 %collective-permute-start.5 = (bf16[1,72,128]{2,1,0:T(8,128)(2,1)S(1)}, bf16[1,72,128]{2,1,0:T(8,128)(2,1)S(1)}, u32[]{:S(2)}, u32[]{:S(2)}) collective-permute-start(bf16[1,72,128]{2,1,0:T(8,128)(2,1)S(1)} %bitcast.11), channel_id=1, source_target_pairs={{0,5},{1,4},{2,7},{3,6},{4,1},{5,0},{6,3},{7,2},{8,13},{9,12},{10,... | collective-permute-start | bytes 55304 | tf_op jit(solution)/shard_map/ppermute | solution.py:39
  9.4 3.7 %copy-start = (bf16[512,64,128]{2,1,0:T(8,128)(2,1)S(1)}, bf16[512,64,128]{2,1,0:T(8,128)(2,1)}, u32[]{:S(2)}) copy-start(bf16[512,64,128]{2,1,0:T(8,128)(2,1)} %p_ref.5) | copy-start | bytes 25165828
  9.4 3.7 %copy-start.1 = (s32[512]{0:T(512)S(1)}, s32[512]{0:T(512)}, u32[]{:S(2)}) copy-start(s32[512]{0:T(512)} %len_hbm.5) | copy-start | bytes 6148
  9.4 5.0 %collective-permute-start.4 = (bf16[3,72,128]{2,1,0:T(8,128)(2,1)S(1)}, bf16[3,72,128]{2,1,0:T(8,128)(2,1)S(1)}, u32[]{:S(2)}, u32[]{:S(2)}) collective-permute-start(bf16[3,72,128]{2,1,0:T(8,128)(2,1)S(1)} %pad_maximum_fusion.1), channel_id=1, source_target_pairs={{0,7},{1,6},{2,5},{3,4},{4,3},{5,2},{6,1},{7,0},{8,15},{9,14},{10,... | collective-permute-start | bytes 165896 | tf_op jit(solution)/shard_map/ppermute | solution.py:39
  12.3 4.1 %collective-permute-start.6 = (bf16[3,72,128]{2,1,0:T(8,128)(2,1)S(1)}, bf16[3,72,128]{2,1,0:T(8,128)(2,1)S(1)}, u32[]{:S(2)}, u32[]{:S(2)}) collective-permute-start(bf16[3,72,128]{2,1,0:T(8,128)(2,1)S(1)} %pad_maximum_fusion.1), channel_id=1, source_target_pairs={{0,5},{1,4},{2,7},{3,6},{4,1},{5,0},{6,3},{7,2},{8,13},{9,12},{10,... | collective-permute-start | bytes 165896 | tf_op jit(solution)/shard_map/ppermute | solution.py:39
  12.3 4.1 %collective-permute-start.7 = (bf16[4,72,128]{2,1,0:T(8,128)(2,1)S(1)}, bf16[4,72,128]{2,1,0:T(8,128)(2,1)S(1)}, u32[]{:S(2)}, u32[]{:S(2)}) collective-permute-start(bf16[4,72,128]{2,1,0:T(8,128)(2,1)S(1)} %pad_maximum_fusion.block_ref.g_ref), channel_id=1, source_target_pairs={{0,3},{1,2},{2,1},{3,0},{4,7},{5,6},{6,5},{7,4},{8,11},{9,10},{10,... | collective-permute-start | bytes 221192 | tf_op jit(solution)/shard_map/ppermute | solution.py:39
  16.5 1.7 %collective-permute-start.8 = (bf16[16,72,128]{2,1,0:T(8,128)(2,1)S(1)}, bf16[16,72,128]{2,1,0:T(8,128)(2,1)S(1)}, u32[]{:S(2)}, u32[]{:S(2)}) collective-permute-start(bf16[16,72,128]{2,1,0:T(8,128)(2,1)S(1)} %constant_dynamic-update-slice_fusion.g_ref), channel_id=1, source_target_pairs={{0,1},{1,0},{2,3},{3,2},{4,5},{5,4},{6,7},{7,6},{8,9},{9,8},{10,11... | collective-permute-start | bytes 884744 | tf_op jit(solution)/shard_map/ppermute | solution.py:260

commit v3 on v2

--- a/solution.py
+++ b/solution.py
@@ -23,7 +23,7 @@
 
 
 def order_of(stage):
-    return (1, 3, 2) if stage == 0 else (3, 2, 1)
+    return (2, 3, 1) if stage == 0 else (3, 2, 1)
 
 
 def flips_of(stages):
@@ -49,10 +49,11 @@
     line, others, marked = lax.optimization_barrier((line, others, mark(line, 2**34) + marked))
     late = [send(others, far, digit) for digit in soon]
     parts = [part for pair in zip(early, late) for part in pair] + [send(line, far, last)]
-    block = jnp.concatenate([line] + parts, axis=0)
+    rest = jnp.concatenate(parts, axis=0)
     for stage, (shift, size) in enumerate(stages[2:], 2):
-        block = jnp.concatenate([block] + [send(block, shift, digit) for digit in order_of(stage)], axis=0)
-    return line, block, marked
+        block = jnp.concatenate([line, rest], axis=0)
+        rest = jnp.concatenate([rest] + [send(block, shift, digit) for digit in order_of(stage)], axis=0)
+    return line, rest, marked
 
 
 def mark_kernel(block_ref, out_ref):
@@ -111,15 +112,17 @@
     return jnp.concatenate(groups, axis=0).astype(jnp.int32)
 
 
-def score_kernel(cap, places, flips, n_earlier, len_hbm, p_ref, mark_ref, g_ref, *refs):
+def score_kernel(cap, n_sets, flips, n_earlier, len_hbm, p_ref, mark_ref, *refs):
     p_local, ptok, dim = p_ref.shape
     last = n_earlier > 0
+    sets, refs = refs[:n_sets], refs[n_sets:]
+    places = [(g_ref, place) for g_ref in sets for place in range(g_ref.shape[0])]
     earlier, refs = refs[:2 * n_earlier], refs[2 * n_earlier:]
     if last:
         out_ref, best, len_ref, len_sem = refs
     else:
         best, rank_ref, len_ref, len_sem = refs
-    tokens = g_ref.shape[1] - ID_ROWS
+    tokens = sets[0].shape[1] - ID_ROWS
     half = tokens // 2
     pairs = cap // 2
     rows = rows_of(len(places))
@@ -127,7 +130,7 @@
     len_copy = pltpu.make_async_copy(len_hbm, len_ref, len_sem)
     len_copy.start()
 
-    ids = ids_of([g_ref[place, tokens:tokens + ID_ROWS, :] for place in places])
+    ids = ids_of([g_ref[place, tokens:tokens + ID_ROWS, :] for g_ref, place in places])
     local = ids - me * p_local
     mine = (ids >= 0) & (local >= 0) & (local < p_local)
     before = lax.broadcasted_iota(jnp.int32, (dim, dim), 0) < lax.broadcasted_iota(jnp.int32, (dim, dim), 1)
@@ -153,7 +156,7 @@
     token = lax.broadcasted_iota(jnp.int32, (8, dim), 0)
     if rows > len(places):
         best[...] = jnp.zeros_like(best)
-    for i, place in enumerate(places):
+    for i, (g_ref, place) in enumerate(places):
         q = g_ref[place, 0:tokens, :]
         zero = jnp.zeros_like(q)
         weight = jnp.concatenate(
@@ -201,10 +204,10 @@
         at += 1
 
 
-def score(count, cap, places, flips, lengths, passages, marked, blocks, earlier=()):
+def score(count, cap, flips, lengths, passages, marked, sets, earlier=()):
     dim = passages.shape[2]
     anywhere, vmem = pl.BlockSpec(memory_space=pl.ANY), pl.BlockSpec(memory_space=pltpu.VMEM)
-    rows = rows_of(len(places))
+    rows = rows_of(sum(blocks.shape[0] for blocks in sets))
     best = ((cap // 2) * rows, dim)
     scratch = [pltpu.SMEM(lengths.shape, jnp.int32), pltpu.SemaphoreType.DMA]
     if earlier:
@@ -214,13 +217,13 @@
         shapes = [jax.ShapeDtypeStruct(best, jnp.float32), jax.ShapeDtypeStruct((rows, dim), jnp.int32)]
         out_specs = [vmem, vmem]
     return pl.pallas_call(
-        functools.partial(score_kernel, cap, places, flips, len(earlier) // 2),
+        functools.partial(score_kernel, cap, len(sets), flips, len(earlier) // 2),
         out_shape=shapes,
-        in_specs=[anywhere, vmem, anywhere] + [vmem] * (1 + len(earlier)),
+        in_specs=[anywhere, vmem, anywhere] + [vmem] * (len(sets) + len(earlier)),
         out_specs=out_specs,
         scratch_shapes=scratch,
         compiler_params=pltpu.CompilerParams(vmem_limit_bytes=24 * 1024 * 1024),
-    )(lengths, passages, marked, blocks, *earlier)
+    )(lengths, passages, marked, *sets, *earlier)
 
 
 def sum_kernel(rows_ref, out_ref):
@@ -252,16 +255,17 @@
     )
     stages = stages_of(count)[:-1]
     sibling = [(d, d ^ 1) for d in range(count)]
-    line, blocks, marked = gather_blocks(packed[None], stages, count)
+    line, rest, marked = gather_blocks(packed[None], stages, count)
     flips = flips_of(stages)
-    first, every = line.shape[0], len(flips)
-    line_call = score(count, cap, range(first), (), lengths, passages, marked, line)
-    blocks, *line_call = lax.optimization_barrier((blocks, *line_call))
-    others = lax.ppermute(blocks, "dev", sibling)
-    rest_call = score(count, cap, range(first, every), (), lengths, passages, marked, blocks)
+    first = line.shape[0]
+    line_call = score(count, cap, (), lengths, passages, marked, (line,))
+    other_line = lax.ppermute(line, "dev", sibling)
+    rest, other_line, *line_call = lax.optimization_barrier((rest, other_line, *line_call))
+    others = lax.ppermute(rest, "dev", sibling)
+    rest_call = score(count, cap, (), lengths, passages, marked, (rest,))
     devices = (flips[:first], flips[first:], [flip ^ 1 for flip in flips])
     dense = score(
-        count, cap, range(every), devices, lengths, passages, marked, others, (*line_call, *rest_call)
+        count, cap, devices, lengths, passages, marked, (other_line, others), (*line_call, *rest_call)
     )
     back = lax.all_to_all(dense, "dev", split_axis=0, concat_axis=0, tiled=True)
     vmem = pl.BlockSpec(memory_space=pltpu.VMEM)

time: 31.5 us -> 31.4 us (level)
  transfers between devices with their start and end apart: 9 -> 10, of which waited for: 3 -> 3; matrix products, arithmetic and copies ran while one was open for 0% -> 0% of each run, Pallas kernels for 7% -> 7%
where the time goes in v3:
time: 31.4 us; the launch traced here: 31.2 us
  starting transfers between devices  12 us (38%)
  blocking collectives  10.8 us (34%)
  Pallas kernels  5.29 us (17%)
  waiting for transfers between devices  2.82 us (9%)
    ppermute x8, starting transfers between devices, send(): return lax.ppermute(block, 'dev', [(d, d ^ flip) for d in range(count)])  11.7 us
    all_to_all x1, blocking collectives, on_device(): back = lax.all_to_all(dense, 'dev', split_axis=0, concat_axis=0, tiled=True)  10.8 us
    pallas_call x3, Pallas kernels, score(): pl.pallas_call(functools.partial(score_kernel, cap, len(sets), flips, len...  3.86 us
    ppermute x8, waiting for transfers between devices, send(): return lax.ppermute(block, 'dev', [(d, d ^ flip) for d in range(count)])  2.81 us
    pallas_call x1, Pallas kernels, on_device(): pl.pallas_call(pack_kernel, out_shape=jax.ShapeDtypeStruct((rows + ID_ROW...  0.78 us
    pallas_call x1, Pallas kernels, on_device(): pl.pallas_call(sum_kernel, out_shape=jax.ShapeDtypeStruct((q_local, cand)...  0.64 us
  transfers between devices with their start and end apart: 10, of which 3 were waited for; matrix products, arithmetic and copies ran while one was open for 0% of the time, Pallas kernels for 7%

profile of v3, /device:TPU:0, one launch (start us, length us, event | category | flops | bytes accessed | tf_op | source)
XLA Modules:
  0.0 31.2 jit_solution(14901305863360103296)
XLA Ops:
  0.0 0.8 %shard_map.46 = bf16[72,128]{1,0:T(8,128)(2,1)S(1)} custom-call(bf16[64,128]{1,0:T(8,128)(2,1)} %bitcast.15, s32[2,64]{1,0:T(2,128)} %c_hbm.1), custom_call_target="tpu_custom_call" | custom-call | tf_op jit(solution)/shard_map/pallas_call | solution.py:245
  0.8 3.5 %collective-permute-start = (bf16[1,72,128]{2,1,0:T(8,128)(2,1)S(1)}, bf16[1,72,128]{2,1,0:T(8,128)(2,1)S(1)}, u32[]{:S(2)}, u32[]{:S(2)}) collective-permute-start(bf16[1,72,128]{2,1,0:T(8,128)(2,1)S(1)} %bitcast.6), channel_id=1, source_target_pairs={{0,17},{1,16},{2,19},{3,18},{4,21},{5,20},{6,23},{7,22},{8,25},{9,... | collective-permute-start | bytes 55304 | tf_op jit(solution)/shard_map/ppermute | solution.py:39
  4.3 1.6 %collective-permute-start.1 = (bf16[1,72,128]{2,1,0:T(8,128)(2,1)S(1)}, bf16[1,72,128]{2,1,0:T(8,128)(2,1)S(1)}, u32[]{:S(2)}, u32[]{:S(2)}) collective-permute-start(bf16[1,72,128]{2,1,0:T(8,128)(2,1)S(1)} %bitcast.7), channel_id=1, source_target_pairs={{0,25},{1,24},{2,27},{3,26},{4,29},{5,28},{6,31},{7,30},{8,17},{9,... | collective-permute-start | bytes 55304 | tf_op jit(solution)/shard_map/ppermute | solution.py:39
  6.0 0.2 collective-permute-start.2
  6.2 2.0 %collective-permute-start.3 = (bf16[1,72,128]{2,1,0:T(8,128)(2,1)S(1)}, bf16[1,72,128]{2,1,0:T(8,128)(2,1)S(1)}, u32[]{:S(2)}, u32[]{:S(2)}) collective-permute-start(bf16[1,72,128]{2,1,0:T(8,128)(2,1)S(1)} %bitcast.10), channel_id=1, source_target_pairs={{0,7},{1,6},{2,5},{3,4},{4,3},{5,2},{6,1},{7,0},{8,15},{9,14},{10,... | collective-permute-start | bytes 55304 | tf_op jit(solution)/shard_map/ppermute | solution.py:39
  8.2 0.7 %collective-permute-start.5 = (bf16[1,72,128]{2,1,0:T(8,128)(2,1)S(1)}, bf16[1,72,128]{2,1,0:T(8,128)(2,1)S(1)}, u32[]{:S(2)}, u32[]{:S(2)}) collective-permute-start(bf16[1,72,128]{2,1,0:T(8,128)(2,1)S(1)} %bitcast.11), channel_id=1, source_target_pairs={{0,5},{1,4},{2,7},{3,6},{4,1},{5,0},{6,3},{7,2},{8,13},{9,12},{10,... | collective-permute-start | bytes 55304 | tf_op jit(solution)/shard_map/ppermute | solution.py:39
  8.9 0.0 collective-permute-done
  8.9 0.5 %collective-permute-done.1 = bf16[1,72,128]{2,1,0:T(8,128)(2,1)S(1)} collective-permute-done((bf16[1,72,128]{2,1,0:T(8,128)(2,1)S(1)}, bf16[1,72,128]{2,1,0:T(8,128)(2,1)S(1)}, u32[]{:S(2)}, u32[]{:S(2)}) %collective-permute-start.1) | collective-permute-done | bytes 18464 | tf_op jit(solution)/shard_map/ppermute | solution.py:39
  9.3 0.0 collective-permute-done.2
  9.4 0.0 copy-start
  9.4 0.0 copy-start.1
  9.4 2.9 %collective-permute-start.4 = (bf16[3,72,128]{2,1,0:T(8,128)(2,1)S(1)}, bf16[3,72,128]{2,1,0:T(8,128)(2,1)S(1)}, u32[]{:S(2)}, u32[]{:S(2)}) collective-permute-start(bf16[3,72,128]{2,1,0:T(8,128)(2,1)S(1)} %pad_maximum_fusion.1), channel_id=1, source_target_pairs={{0,7},{1,6},{2,5},{3,4},{4,3},{5,2},{6,1},{7,0},{8,15},{9,14},{10,... | collective-permute-start | bytes 165896 | tf_op jit(solution)/shard_map/ppermute | solution.py:39
  12.3 0.0 collective-permute-start.6
  12.3 0.8 %collective-permute-start.7 = (bf16[4,72,128]{2,1,0:T(8,128)(2,1)S(1)}, bf16[4,72,128]{2,1,0:T(8,128)(2,1)S(1)}, u32[]{:S(2)}, u32[]{:S(2)}) collective-permute-start(bf16[4,72,128]{2,1,0:T(8,128)(2,1)S(1)} %pad_maximum_fusion.block_ref.refs_0_), channel_id=1, source_target_pairs={{0,3},{1,2},{2,1},{3,0},{4,7},{5,6},{6,5},{7,4},{8,11},{9,10},{10,... | collective-permute-start | bytes 221192 | tf_op jit(solution)/shard_map/ppermute | solution.py:39
  13.0 0.0 collective-permute-done.3
  13.0 0.0 collective-permute-start.8
  13.1 0.0 copy-done
  13.1 0.0 copy-done.1
  13.1 1.0 %shard_map.49 = (f32[32,128]{1,0:T(8,128)S(1)}, s32[8,128]{1,0:T(8,128)S(1)}) custom-call(s32[512]{0:T(512)S(1)} %copy-done.1, bf16[512,64,128]{2,1,0:T(8,128)(2,1)S(1)} %copy-done, f32[8,128]{1,0:T(8,128)S(1)} %add.3.mark_ref, bf16[4,72,128]{2,1,0:T(8,128)(2,1)S(1)} %pad_maximum_fusion.block_ref.refs_0_), custom_call_target="tpu_custom_call" | custom-call | tf_op jit(solution)/shard_map/pallas_call | solution.py:219
  14.0 0.4 %collective-permute-done.4 = bf16[3,72,128]{2,1,0:T(8,128)(2,1)S(1)} collective-permute-done((bf16[3,72,128]{2,1,0:T(8,128)(2,1)S(1)}, bf16[3,72,128]{2,1,0:T(8,128)(2,1)S(1)}, u32[]{:S(2)}, u32[]{:S(2)}) %collective-permute-start.4) | collective-permute-done | bytes 55328 | tf_op jit(solution)/shard_map/ppermute | solution.py:39
  14.5 0.0 collective-permute-done.5
  14.5 1.9 %collective-permute-done.6 = bf16[3,72,128]{2,1,0:T(8,128)(2,1)S(1)} collective-permute-done((bf16[3,72,128]{2,1,0:T(8,128)(2,1)S(1)}, bf16[3,72,128]{2,1,0:T(8,128)(2,1)S(1)}, u32[]{:S(2)}, u32[]{:S(2)}) %collective-permute-start.6) | collective-permute-done | bytes 55328 | tf_op jit(solution)/shard_map/ppermute | solution.py:39
  16.4 0.0 collective-permute-done.7
  16.5 0.0 collective-permute-done.8.refs_0_
  16.5 0.3 collective-permute-start.9
  16.8 1.3 %shard_map.50 = (f32[64,128]{1,0:T(8,128)S(1)}, s32[16,128]{1,0:T(8,128)S(1)}) custom-call(s32[512]{0:T(512)S(1)} %copy-done.1, bf16[512,64,128]{2,1,0:T(8,128)(2,1)S(1)} %copy-done, f32[8,128]{1,0:T(8,128)S(1)} %add.3.mark_ref, bf16[12,72,128]{2,1,0:T(8,128)(2,1)S(1)} %constant_dynamic-update-slice_fusion.refs_0_), custom_call_target="tpu_custom_call" | custom-call | tf_op jit(solution)/shard_map/pallas_call | solution.py:219
  18.1 0.0 collective-permute-done.9.refs_1_
  18.1 1.6 %shard_map.51 = f32[32,128]{1,0:T(8,128)S(1)} custom-call(s32[512]{0:T(512)S(1)} %copy-done.1, bf16[512,64,128]{2,1,0:T(8,128)(2,1)S(1)} %copy-done, f32[8,128]{1,0:T(8,128)S(1)} %add.3.mark_ref, bf16[4,72,128]{2,1,0:T(8,128)(2,1)S(1)} %collective-permute-done.8.refs_0_, bf16[12,72,128]{2,1,0:T(8,128)(2,1)S(1)} %collective-permute-done.9.refs_1_, ...), custom_call_target="tpu_custom_call" | custom-call | tf_op jit(solution)/shard_map/pallas_call | solution.py:219
  19.7 10.8 %all_to_all.11 = f32[32,1,128]{2,1,0:T(1,128)S(1)} all-to-all(f32[32,1,128]{2,1,0:T(1,128)S(1)} %bitcast.13), channel_id=1, replica_groups=mesh['dev'=32] {'dev'}, dimensions={0} | all-to-all | bytes 32768 | tf_op jit(solution)/shard_map/all_to_all | solution.py:270
  30.5 0.6 %shard_map.52 = f32[2,64]{1,0:T(2,128)} custom-call(f32[32,128]{1,0:T(8,128)S(1)} %bitcast.14), custom_call_target="tpu_custom_call" | custom-call | tf_op jit(solution)/shard_map/pallas_call | solution.py:272
  (10 shorter events, 0.1 us)
Async XLA Ops:
  0.8 8.1 %collective-permute-start = (bf16[1,72,128]{2,1,0:T(8,128)(2,1)S(1)}, bf16[1,72,128]{2,1,0:T(8,128)(2,1)S(1)}, u32[]{:S(2)}, u32[]{:S(2)}) collective-permute-start(bf16[1,72,128]{2,1,0:T(8,128)(2,1)S(1)} %bitcast.6), channel_id=1, source_target_pairs={{0,17},{1,16},{2,19},{3,18},{4,21},{5,20},{6,23},{7,22},{8,25},{9,... | collective-permute-start | bytes 55304 | tf_op jit(solution)/shard_map/ppermute | solution.py:39
  4.3 5.0 %collective-permute-start.1 = (bf16[1,72,128]{2,1,0:T(8,128)(2,1)S(1)}, bf16[1,72,128]{2,1,0:T(8,128)(2,1)S(1)}, u32[]{:S(2)}, u32[]{:S(2)}) collective-permute-start(bf16[1,72,128]{2,1,0:T(8,128)(2,1)S(1)} %bitcast.7), channel_id=1, source_target_pairs={{0,25},{1,24},{2,27},{3,26},{4,29},{5,28},{6,31},{7,30},{8,17},{9,... | collective-permute-start | bytes 55304 | tf_op jit(solution)/shard_map/ppermute | solution.py:39
  6.0 3.4 %collective-permute-start.2 = (bf16[1,72,128]{2,1,0:T(8,128)(2,1)S(1)}, bf16[1,72,128]{2,1,0:T(8,128)(2,1)S(1)}, u32[]{:S(2)}, u32[]{:S(2)}) collective-permute-start(bf16[1,72,128]{2,1,0:T(8,128)(2,1)S(1)} %bitcast.8), channel_id=1, source_target_pairs={{0,9},{1,8},{2,11},{3,10},{4,13},{5,12},{6,15},{7,14},{8,1},{9,0},... | collective-permute-start | bytes 55304 | tf_op jit(solution)/shard_map/ppermute | solution.py:39
  6.2 6.9 %collective-permute-start.3 = (bf16[1,72,128]{2,1,0:T(8,128)(2,1)S(1)}, bf16[1,72,128]{2,1,0:T(8,128)(2,1)S(1)}, u32[]{:S(2)}, u32[]{:S(2)}) collective-permute-start(bf16[1,72,128]{2,1,0:T(8,128)(2,1)S(1)} %bitcast.10), channel_id=1, source_target_pairs={{0,7},{1,6},{2,5},{3,4},{4,3},{5,2},{6,1},{7,0},{8,15},{9,14},{10,... | collective-permute-start | bytes 55304 | tf_op jit(solution)/shard_map/ppermute | solution.py:39
  8.2 6.3 %collective-permute-start.5 = (bf16[1,72,128]{2,1,0:T(8,128)(2,1)S(1)}, bf16[1,72,128]{2,1,0:T(8,128)(2,1)S(1)}, u32[]{:S(2)}, u32[]{:S(2)}) collective-permute-start(bf16[1,72,128]{2,1,0:T(8,128)(2,1)S(1)} %bitcast.11), channel_id=1, source_target_pairs={{0,5},{1,4},{2,7},{3,6},{4,1},{5,0},{6,3},{7,2},{8,13},{9,12},{10,... | collective-permute-start | bytes 55304 | tf_op jit(solution)/shard_map/ppermute | solution.py:39
  9.4 3.7 %copy-start = (bf16[512,64,128]{2,1,0:T(8,128)(2,1)S(1)}, bf16[512,64,128]{2,1,0:T(8,128)(2,1)}, u32[]{:S(2)}) copy-start(bf16[512,64,128]{2,1,0:T(8,128)(2,1)} %p_ref.5) | copy-start | bytes 25165828
  9.4 3.7 %copy-start.1 = (s32[512]{0:T(512)S(1)}, s32[512]{0:T(512)}, u32[]{:S(2)}) copy-start(s32[512]{0:T(512)} %len_hbm.5) | copy-start | bytes 6148
  9.4 5.0 %collective-permute-start.4 = (bf16[3,72,128]{2,1,0:T(8,128)(2,1)S(1)}, bf16[3,72,128]{2,1,0:T(8,128)(2,1)S(1)}, u32[]{:S(2)}, u32[]{:S(2)}) collective-permute-start(bf16[3,72,128]{2,1,0:T(8,128)(2,1)S(1)} %pad_maximum_fusion.1), channel_id=1, source_target_pairs={{0,7},{1,6},{2,5},{3,4},{4,3},{5,2},{6,1},{7,0},{8,15},{9,14},{10,... | collective-permute-start | bytes 165896 | tf_op jit(solution)/shard_map/ppermute | solution.py:39
  12.3 4.1 %collective-permute-start.6 = (bf16[3,72,128]{2,1,0:T(8,128)(2,1)S(1)}, bf16[3,72,128]{2,1,0:T(8,128)(2,1)S(1)}, u32[]{:S(2)}, u32[]{:S(2)}) collective-permute-start(bf16[3,72,128]{2,1,0:T(8,128)(2,1)S(1)} %pad_maximum_fusion.1), channel_id=1, source_target_pairs={{0,5},{1,4},{2,7},{3,6},{4,1},{5,0},{6,3},{7,2},{8,13},{9,12},{10,... | collective-permute-start | bytes 165896 | tf_op jit(solution)/shard_map/ppermute | solution.py:39
  12.3 4.1 %collective-permute-start.7 = (bf16[4,72,128]{2,1,0:T(8,128)(2,1)S(1)}, bf16[4,72,128]{2,1,0:T(8,128)(2,1)S(1)}, u32[]{:S(2)}, u32[]{:S(2)}) collective-permute-start(bf16[4,72,128]{2,1,0:T(8,128)(2,1)S(1)} %pad_maximum_fusion.block_ref.refs_0_), channel_id=1, source_target_pairs={{0,3},{1,2},{2,1},{3,0},{4,7},{5,6},{6,5},{7,4},{8,11},{9,10},{10,... | collective-permute-start | bytes 221192 | tf_op jit(solution)/shard_map/ppermute | solution.py:39
  13.0 3.4 %collective-permute-start.8 = (bf16[4,72,128]{2,1,0:T(8,128)(2,1)S(1)}, bf16[4,72,128]{2,1,0:T(8,128)(2,1)S(1)}, u32[]{:S(2)}, u32[]{:S(2)}) collective-permute-start(bf16[4,72,128]{2,1,0:T(8,128)(2,1)S(1)} %pad_maximum_fusion.block_ref.refs_0_), channel_id=1, source_target_pairs={{0,1},{1,0},{2,3},{3,2},{4,5},{5,4},{6,7},{7,6},{8,9},{9,8},{10,11... | collective-permute-start | bytes 221192 | tf_op jit(solution)/shard_map/ppermute | solution.py:262
  16.5 1.6 %collective-permute-start.9 = (bf16[12,72,128]{2,1,0:T(8,128)(2,1)S(1)}, bf16[12,72,128]{2,1,0:T(8,128)(2,1)S(1)}, u32[]{:S(2)}, u32[]{:S(2)}) collective-permute-start(bf16[12,72,128]{2,1,0:T(8,128)(2,1)S(1)} %constant_dynamic-update-slice_fusion.refs_0_), channel_id=1, source_target_pairs={{0,1},{1,0},{2,3},{3,2},{4,5},{5,4},{6,7},{7,6},{8,9},{9,8},{10,11... | collective-permute-start | bytes 663560 | tf_op jit(solution)/shard_map/ppermute | solution.py:264
